TPU v7x, 512 devices: a whole 4x8x8 slice. The times are simulated.
512 devices in a mesh: samp: 32 (over z, x_hi, core), par: 16 (over x_lo, y).
Axes of the slice: x: 4 (x_hi: 2, x_lo: 2; x = x_hi * 2 + x_lo), y: 8, z: 8, core: 2. Of those that a mesh axis runs over, the one named last changes fastest.
Arguments:
- activations: bfloat16 [512, 2, 64, 256], P('samp'), may hold values from 0 to 2
- cotangents: bfloat16 [512, 2, 64, 256], P('samp', None, 'par'), may hold values from -0.029907227 to 0.099609375
- energies: float32 [512], P('samp'), may hold values from -3 to -1
Outputs:
- update: float32 [64, 1152], P('par')
- coeffs: float32 [512], P('samp')
All inputs are finite; a program needn't handle non-finite values.
Results may differ from a plain program's by a relative error of at most 0.0034.
Values may be sent and summed in bfloat16 or wider, within the bound.
A program may use at most 64 MiB of HBM per device.

v0:
```python
import math
import jax
import jax.numpy as jnp
from jax import lax
from jax.sharding import PartitionSpec as P

C = 64
SIDE = 16
LAYERS = 2
reg_shift = 0.1


def sample_grads(activations, cotangents):
    sample_count, layer_count, channels, site_count = activations.shape
    owned_out = cotangents.shape[2]
    field = cotangents.reshape(sample_count, layer_count, owned_out, SIDE, SIDE)
    shifted = [
        jnp.roll(field, (row_step - 1, col_step - 1), axis=(3, 4))
        for row_step in range(3)
        for col_step in range(3)
    ]
    stacked = jnp.stack(shifted, axis=3).reshape(
        sample_count, layer_count, owned_out * 9, site_count
    )
    grads = jnp.einsum("slkx,slix->slki", stacked, activations, preferred_element_type=jnp.float32)
    grads = grads.reshape(sample_count, layer_count, owned_out, 9, channels).transpose(
        0, 2, 1, 4, 3
    )
    return grads.reshape(sample_count, owned_out * layer_count * channels * 9)


def contract(left_rows, right_rows):
    return lax.dot_general(
        left_rows, right_rows, (((1,), (1,)), ((), ())), preferred_element_type=jnp.float32
    )


def solve_system(gram, dev_all, total):
    regular = gram + reg_shift * jnp.eye(total, dtype=jnp.float32)
    factor = jnp.linalg.cholesky(regular)
    forward = lax.linalg.triangular_solve(factor, dev_all[:, None], left_side=True, lower=True)
    return lax.linalg.triangular_solve(
        factor, forward, left_side=True, lower=True, transpose_a=True
    )[:, 0]


def local(activations, cotangents, energies):
    grads = sample_grads(activations, cotangents)
    local_count = grads.shape[0]
    members = lax.axis_size("samp")
    position = lax.axis_index("samp")
    total = members * local_count
    params_all = LAYERS * C * C * 9
    scale = -math.sqrt(params_all / total)
    col_sums, energy_sum = lax.psum((jnp.sum(grads, axis=0), jnp.sum(energies)), "samp")
    centered = ((grads - col_sums / total) * (1.0 / math.sqrt(params_all))).astype(jnp.bfloat16)
    deviation = energies - energy_sum / total
    partial_value = contract(centered, lax.all_gather(centered, "samp", axis=0, tiled=True))
    summed = lax.psum(partial_value, "par")
    gram, dev_column = (
        lax.all_gather(summed, "samp", axis=0, tiled=True),
        lax.all_gather(deviation[:, None], "samp", axis=0, tiled=True),
    )
    dev_all = dev_column[:, 0]
    coeffs = solve_system(gram, dev_all, total)
    local_coeffs = lax.dynamic_slice_in_dim(coeffs, position * local_count, local_count)
    term = jnp.dot(
        local_coeffs[None, :], centered.astype(jnp.float32), precision=lax.Precision.HIGHEST
    )[0]
    summed_term = lax.psum(term, "samp")
    update = scale * summed_term
    return (update.reshape(cotangents.shape[2], -1), local_coeffs)


def solution(mesh):
    return jax.shard_map(
        local,
        mesh=mesh,
        in_specs=(P("samp", None, None, None), P("samp", None, "par", None), P("samp")),
        out_specs=(P("par", None), P("samp")),
        check_vma=False,
    )
```

profile of v0, /device:TPU:8, one launch (start us, length us, event | category | flops | bytes accessed | tf_op | source)
XLA Modules:
  0.0 767.5 jit_solution(1295712559334834222)
XLA Ops:
  7.2 1.3 reshape.131
  9.5 1.0 fusion.74
  10.5 1.2 fusion.75
  11.7 1.2 fusion.72
  12.9 1.2 fusion.73
  15.0 2.5 fusion.15
  17.5 0.9 bitcast_dynamic-update-slice_fusion.2
  18.5 1.1 fusion.16
  19.6 0.6 pad_maximum_fusion.1
  20.2 0.9 fusion.20
  21.1 0.9 copy_dynamic-update-slice_fusion
  22.0 0.9 fusion.19
  22.8 1.1 fusion.17
  24.0 0.9 bitcast_dynamic-update-slice_fusion.1
  24.8 1.1 fusion.18
  25.9 6.1 reshape.132
  32.7 2.7 copy.66
  35.7 0.6 reduce_sum.22
  36.5 76.6 %psum.30 = f32[]{:T(128)} all-reduce(f32[]{:T(128)} %reduce_sum.22), channel_id=1, replica_groups=mesh['samp'=32,'par'=16] {'samp'}, use_global_device_ids=true, to_apply=%region_12.13 | all-reduce | flops 1 | bytes 8 | tf_op jit(solution)/shard_map/psum | solution.py:55
  113.1 1.3 dynamic-slice.4
  115.8 128.5 %all-reduce.2 = (f32[4608]{0:T(1024)S(1)}, f32[512]{0:T(512)S(1)}) all-reduce(f32[4608]{0:T(1024)S(1)} %reduce_sum.21, f32[512]{0:T(512)S(1)} %subtract_dynamic-update-slice_fusion), channel_id=1, replica_groups=mesh['samp'=32,'par'=16] {'samp'}, use_global_device_ids=true, to_apply=%region_1.2 | all-reduce | flops 5120 | bytes 40960 | tf_op jit(solution)/shard_map/psum | solution.py:55
  244.3 3.4 reshape.134
  247.6 0.7 multiply_convert_fusion.1
  248.4 88.7 %all-gather.4.cloned.1.call-done = bf16[512,4608]{1,0:T(8,128)(2,1)} async-done(((bf16[16,4608]{1,0:T(8,128)(2,1)}), bf16[512,4608]{1,0:T(8,128)(2,1)}) %all-gather.4.cloned.1.call-update) | async-done | bytes 4718608 | tf_op jit(solution)/shard_map/all_gather | solution.py:58
  337.2 3.7 fusion.76
  340.9 58.7 %psum.29 = f32[16,512]{1,0:T(8,128)} all-reduce(f32[16,512]{1,0:T(8,128)S(1)} %fusion.76), channel_id=1, replica_groups=mesh['samp'=32,'par'=16] {'par'}, use_global_device_ids=true, to_apply=%region_2.3 | all-reduce | flops 8192 | bytes 65536 | tf_op jit(solution)/shard_map/psum | solution.py:59
  400.1 1.1 copy.79
  401.2 2.8 convert_element_type.12
  404.1 75.9 %all-gather.6.cloned.1.call-done = f32[512,512]{1,0:T(8,128)} async-done(((f32[16,512]{1,0:T(8,128)}), f32[512,512]{1,0:T(8,128)}) %all-gather.6.cloned.1.call-update) | async-done | bytes 1048592 | tf_op jit(solution)/shard_map/all_gather | solution.py:61
  480.0 1.6 copy.68
  481.5 1.1 select_add_fusion
  482.6 1.6 copy.69
  484.4 1.0 copy-done.1
  485.4 11.7 %cholesky.103 = f32[128,128]{1,0:T(8,128)S(1)} custom-call(f32[128,128]{1,0:T(8,128)S(1)} %cholesky.263), custom_call_target="Cholesky" | custom-call | tf_op jit(solution)/shard_map/jit(cholesky)/cholesky | solution.py:40
  497.2 9.8 %custom-call.32 = f32[1,128,128]{1,2,0:T(8,128)S(1)} custom-call(f32[1,128,128]{2,1,0:T(8,128)S(1)} %get-tuple-element.55), custom_call_target="InvertDiagBlocksLowerTriangular" | custom-call | tf_op jit(solution)/shard_map/jit(cholesky)/cholesky | solution.py:40
  507.0 1.2 fusion.25
  508.2 1.3 convolution_subtract_fusion
  509.5 11.7 %cholesky.215 = f32[128,128]{1,0:T(8,128)S(1)} custom-call(f32[128,128]{1,0:T(8,128)S(1)} %cholesky.267), custom_call_target="Cholesky" | custom-call | tf_op jit(solution)/shard_map/jit(cholesky)/cholesky | solution.py:40
  521.7 10.0 %custom-call.33 = f32[1,128,128]{1,2,0:T(8,128)S(1)} custom-call(f32[1,128,128]{2,1,0:T(8,128)S(1)} %get-tuple-element.53), custom_call_target="InvertDiagBlocksLowerTriangular" | custom-call | tf_op jit(solution)/shard_map/jit(cholesky)/cholesky | solution.py:40
  532.1 1.5 convolution_subtract_fusion.1
  533.6 11.7 %cholesky.236 = f32[128,128]{1,0:T(8,128)S(1)} custom-call(f32[128,128]{1,0:T(8,128)S(1)} %cholesky.272), custom_call_target="Cholesky" | custom-call | tf_op jit(solution)/shard_map/jit(cholesky)/cholesky | solution.py:40
  545.4 9.8 %custom-call.34 = f32[1,128,128]{1,2,0:T(8,128)S(1)} custom-call(f32[1,128,128]{2,1,0:T(8,128)S(1)} %get-tuple-element.51), custom_call_target="InvertDiagBlocksLowerTriangular" | custom-call | tf_op jit(solution)/shard_map/jit(cholesky)/cholesky | solution.py:40
  555.6 1.3 convolution_subtract_fusion.2
  556.9 12.0 %cholesky.253 = f32[128,128]{1,0:T(8,128)S(1)} custom-call(f32[128,128]{1,0:T(8,128)S(1)} %convolution_subtract_fusion.2), custom_call_target="Cholesky" | custom-call | tf_op jit(solution)/shard_map/jit(cholesky)/cholesky | solution.py:40
  569.0 0.7 compare_reduce_fusion.2
  569.7 0.6 compare_reduce_fusion.3
  570.3 0.6 compare_reduce_fusion.1
  571.0 0.7 compare_reduce_fusion
  574.3 11.3 %while.1 = (s32[]{:T(128)}, f32[512,512]{0,1:T(8,128)S(1)}, s32[4,2]{0,1:T(2,128)S(1)}, f32[4,128,128]{2,1,0:T(8,128)}, s32[]{:T(128)}) while((s32[]{:T(128)}, f32[512,512]{0,1:T(8,128)S(1)}, s32[4,2]{0,1:T(2,128)S(1)}, f32[4,128,128]{2,1,0:T(8,128)}, s32[]{:T(128)}) %tuple.39), condition=%wide.while_cond, body=%wide.while_body.sunk | while | flops 2 | bytes 393829 | solution.py:42
  574.4 0.6 fusion.100
  575.0 1.4 dynamic-slice.9
  576.5 0.6 bitcast_dynamic-update-slice_fusion.4
  577.2 0.6 fusion.100
  577.8 1.4 dynamic-slice.9
  579.4 0.6 bitcast_dynamic-update-slice_fusion.4
  580.0 0.6 fusion.100
  580.6 1.4 dynamic-slice.9
  582.2 0.6 bitcast_dynamic-update-slice_fusion.4
  582.9 0.6 fusion.100
  583.5 1.4 dynamic-slice.9
  585.0 0.6 bitcast_dynamic-update-slice_fusion.4
  585.6 40.1 %custom-call.35 = f32[4,128,128]{1,2,0:T(8,128)S(1)} custom-call(f32[4,128,128]{2,1,0:T(8,128)} %get-tuple-element.9), custom_call_target="InvertDiagBlocksLowerTriangular" | custom-call | tf_op jit(solution)/shard_map/triangular_solve | solution.py:42
  629.0 130.5 %psum.31 = f32[4608]{0:T(1024)S(1)} all-reduce(f32[4608]{0:T(1024)S(1)} %convolution_reduce_fusion), channel_id=1, replica_groups=mesh['samp'=32,'par'=16] {'samp'}, use_global_device_ids=true, to_apply=%region_13.14 | all-reduce | flops 4608 | bytes 36864 | tf_op jit(solution)/shard_map/psum | solution.py:70
  759.6 0.6 reshape.144
  (89 shorter events, 9.3 us)
Async XLA Ops:
  7.2 24.9 %copy-start = (bf16[16,2,64,256]{3,2,1,0:T(8,128)(2,1)S(1)}, bf16[16,2,64,256]{3,2,1,0:T(8,128)(2,1)}, u32[]{:S(2)}) copy-start(bf16[16,2,64,256]{3,2,1,0:T(8,128)(2,1)} %param.3) | copy-start | bytes 3145732
  7.2 330.0 %all-gather.4.cloned.1.call-start = ((), (), s32[]{:S(2)}) async-start(), calls=%async_computation | async-start | bytes 4866048 | tf_op jit(solution)/shard_map/all_gather | solution.py:58
  9.5 4.6 copy-start.7
  14.5 4.0 copy-start.2
  14.5 5.1 copy-start.3
  14.5 5.1 copy-start.4
  14.5 5.1 copy-start.5
  14.5 5.1 copy-start.6
  32.0 3.7 copy-start.9
  248.4 231.6 %all-gather.6.cloned.1.call-start = ((), (), s32[]{:S(2)}) async-start(), calls=%async_computation.1 | async-start | bytes 1081344 | tf_op jit(solution)/shard_map/all_gather | solution.py:61
  484.4 1.0 copy-start.1
  628.8 131.4 %copy-start.8 = (f32[16,1]{0,1:T(1,128)}, f32[16,1]{0,1:T(1,128)S(1)}, u32[]{:S(2)}) copy-start(f32[16,1]{0,1:T(1,128)S(1)} %fusion.59) | copy-start | bytes 196
Sparse Core Ops, SparseCore 0:
  248.5 88.6 all-gather.3
  399.8 80.1 all-gather.5
where the time goes:
time: 777 us; the launch traced here: 767 us
  blocking collectives  394 us (51%)
  waiting for transfers between devices  165 us (21%)
  other arithmetic  130 us (17%)
  local copies, waits for them, and re-layouts  46.6 us (6%)
  between operations  18.8 us (2%)
  matrix products  13.2 us (2%)
    psum x2, blocking collectives, local(): lax.psum((jnp.sum(grads, axis=0), jnp.sum(energies)), 'samp')  205 us
    psum x1, blocking collectives, local(): summed_term = lax.psum(term, 'samp')  131 us
    all_gather x1, waiting for transfers between devices, local(): lax.all_gather(centered, 'samp', axis=0, tiled=True)  88.7 us
    another operation x15, other arithmetic, solve_system(): factor = jnp.linalg.cholesky(regular)  79.5 us
    all_gather x1, waiting for transfers between devices, local(): lax.all_gather(summed, 'samp', axis=0, tiled=True)  75.9 us
    psum x1, blocking collectives, local(): summed = lax.psum(partial_value, 'par')  58.7 us
    another operation x4, other arithmetic, solve_system(): lax.linalg.triangular_solve(factor, forward, left_side=True, lower=True,...  40.4 us
  transfers between devices with their start and end apart: 2, of which 2 were waited for; matrix products, arithmetic and copies ran while one was open for 1% of the time, Pallas kernels for 0%

commit v1 on v0

--- a/solution.py
+++ b/solution.py
@@ -8,6 +8,13 @@
 SIDE = 16
 LAYERS = 2
 reg_shift = 0.1
+
+
+def gather_over(x, axis, d):
+    size = lax.axis_size(axis)
+    pieces = jnp.stack([x for _ in range(size)])
+    pieces = lax.all_to_all(pieces, axis, split_axis=0, concat_axis=0)
+    return jnp.concatenate(pieces, axis=d)
 
 
 def sample_grads(activations, cotangents):
@@ -58,7 +65,7 @@
     partial_value = contract(centered, lax.all_gather(centered, "samp", axis=0, tiled=True))
     summed = lax.psum(partial_value, "par")
     gram, dev_column = (
-        lax.all_gather(summed, "samp", axis=0, tiled=True),
+        gather_over(summed, "samp", 0),
         lax.all_gather(deviation[:, None], "samp", axis=0, tiled=True),
     )
     dev_all = dev_column[:, 0]

time: 777 us -> 734 us (0.945)
  the two profiles are of different devices: /device:TPU:8 before, /device:TPU:2 now
where the time goes in v1:
time: 734 us; the launch traced here: 724 us
  blocking collectives  396 us (54%)
  other arithmetic  130 us (18%)
  waiting for transfers between devices  114 us (16%)
  local copies, waits for them, and re-layouts  47.8 us (7%)
  between operations  18.8 us (3%)
  matrix products  13.2 us (2%)
    psum x2, blocking collectives, local(): lax.psum((jnp.sum(grads, axis=0), jnp.sum(energies)), 'samp')  204 us
    psum x1, blocking collectives, local(): summed_term = lax.psum(term, 'samp')  128 us
    all_gather x1, waiting for transfers between devices, local(): lax.all_gather(centered, 'samp', axis=0, tiled=True)  88.9 us
    another operation x15, other arithmetic, solve_system(): factor = jnp.linalg.cholesky(regular)  79.5 us
    psum x1, blocking collectives, local(): summed = lax.psum(partial_value, 'par')  63.5 us
    another operation x4, other arithmetic, solve_system(): lax.linalg.triangular_solve(factor, forward, left_side=True, lower=True,...  40.4 us
    all_to_all x1, waiting for transfers between devices, gather_over(): pieces = lax.all_to_all(pieces, axis, split_axis=0, concat_axis=0)  24.6 us
  transfers between devices with their start and end apart: 2, of which 2 were waited for; matrix products, arithmetic and copies ran while one was open for 1% of the time, Pallas kernels for 0%

profile of v1, /device:TPU:2, one launch (start us, length us, event | category | flops | bytes accessed | tf_op | source)
XLA Modules:
  0.0 724.0 jit_solution(5381741761960473940)
XLA Ops:
  7.2 1.3 reshape.136
  9.5 1.0 fusion.74
  10.5 1.2 fusion.75
  11.7 1.2 fusion.72
  12.9 1.2 fusion.73
  15.0 2.5 fusion.15
  17.5 0.9 bitcast_dynamic-update-slice_fusion.2
  18.5 1.1 fusion.16
  20.2 0.9 fusion.20
  21.1 0.9 copy_dynamic-update-slice_fusion
  22.0 0.9 fusion.19
  22.8 1.1 fusion.17
  24.0 0.9 bitcast_dynamic-update-slice_fusion.1
  24.8 1.1 fusion.18
  25.9 6.1 reshape.137
  32.7 2.7 copy.66
  35.7 0.6 reduce_sum.22
  36.5 75.7 %psum.30 = f32[]{:T(128)} all-reduce(f32[]{:T(128)} %reduce_sum.22), channel_id=1, replica_groups=mesh['samp'=32,'par'=16] {'samp'}, use_global_device_ids=true, to_apply=%region_12.13 | all-reduce | flops 1 | bytes 8 | tf_op jit(solution)/shard_map/psum | solution.py:62
  112.2 1.3 dynamic-slice.4
  114.9 128.5 %all-reduce.2 = (f32[4608]{0:T(1024)S(1)}, f32[512]{0:T(512)S(1)}) all-reduce(f32[4608]{0:T(1024)S(1)} %reduce_sum.21, f32[512]{0:T(512)S(1)} %subtract_dynamic-update-slice_fusion), channel_id=1, replica_groups=mesh['samp'=32,'par'=16] {'samp'}, use_global_device_ids=true, to_apply=%region_1.2 | all-reduce | flops 5120 | bytes 40960 | tf_op jit(solution)/shard_map/psum | solution.py:62
  243.4 3.4 reshape.139
  246.7 0.7 multiply_convert_fusion.1
  247.5 88.9 %all-gather.3.cloned.1.call-done = bf16[512,4608]{1,0:T(8,128)(2,1)} async-done(((bf16[16,4608]{1,0:T(8,128)(2,1)}), bf16[512,4608]{1,0:T(8,128)(2,1)}) %all-gather.3.cloned.1.call-update) | async-done | bytes 4718608 | tf_op jit(solution)/shard_map/all_gather | solution.py:65
  336.3 3.7 fusion.76
  340.1 63.5 %psum.29 = f32[16,512]{1,0:T(8,128)S(1)} all-reduce(f32[16,512]{1,0:T(8,128)S(1)} %fusion.76), channel_id=1, replica_groups=mesh['samp'=32,'par'=16] {'par'}, use_global_device_ids=true, to_apply=%region_2.3 | all-reduce | flops 8192 | bytes 65536 | tf_op jit(solution)/shard_map/psum | solution.py:66
  403.6 1.2 stack.32
  404.7 4.7 all-to-all-start
  409.9 1.1 copy.79
  411.0 2.8 convert_element_type.12
  413.8 24.6 %all-to-all-done = f32[32,16,512]{2,1,0:T(8,128)} async-done(((f32[32,16,512]{2,1,0:T(8,128)}), f32[32,16,512]{2,1,0:T(8,128)}, u32[]{:S(2)}, u32[]{:S(2)}) %all-to-all-start) | async-done | bytes 1048608 | tf_op jit(solution)/shard_map/all_to_all | solution.py:16
  438.5 1.6 copy.68
  440.0 1.1 select_add_fusion
  441.1 1.6 copy.69
  442.9 1.0 copy-done.1
  443.9 11.7 %cholesky.103 = f32[128,128]{1,0:T(8,128)S(1)} custom-call(f32[128,128]{1,0:T(8,128)S(1)} %cholesky.263), custom_call_target="Cholesky" | custom-call | tf_op jit(solution)/shard_map/jit(cholesky)/cholesky | solution.py:47
  455.7 9.8 %custom-call.32 = f32[1,128,128]{1,2,0:T(8,128)S(1)} custom-call(f32[1,128,128]{2,1,0:T(8,128)S(1)} %get-tuple-element.55), custom_call_target="InvertDiagBlocksLowerTriangular" | custom-call | tf_op jit(solution)/shard_map/jit(cholesky)/cholesky | solution.py:47
  465.5 1.2 fusion.25
  466.7 1.3 convolution_subtract_fusion
  468.0 11.7 %cholesky.215 = f32[128,128]{1,0:T(8,128)S(1)} custom-call(f32[128,128]{1,0:T(8,128)S(1)} %cholesky.267), custom_call_target="Cholesky" | custom-call | tf_op jit(solution)/shard_map/jit(cholesky)/cholesky | solution.py:47
  480.2 10.0 %custom-call.33 = f32[1,128,128]{1,2,0:T(8,128)S(1)} custom-call(f32[1,128,128]{2,1,0:T(8,128)S(1)} %get-tuple-element.53), custom_call_target="InvertDiagBlocksLowerTriangular" | custom-call | tf_op jit(solution)/shard_map/jit(cholesky)/cholesky | solution.py:47
  490.6 1.5 convolution_subtract_fusion.1
  492.1 11.7 %cholesky.236 = f32[128,128]{1,0:T(8,128)S(1)} custom-call(f32[128,128]{1,0:T(8,128)S(1)} %cholesky.272), custom_call_target="Cholesky" | custom-call | tf_op jit(solution)/shard_map/jit(cholesky)/cholesky | solution.py:47
  504.0 9.8 %custom-call.34 = f32[1,128,128]{1,2,0:T(8,128)S(1)} custom-call(f32[1,128,128]{2,1,0:T(8,128)S(1)} %get-tuple-element.51), custom_call_target="InvertDiagBlocksLowerTriangular" | custom-call | tf_op jit(solution)/shard_map/jit(cholesky)/cholesky | solution.py:47
  514.1 1.3 convolution_subtract_fusion.2
  515.4 11.9 %cholesky.253 = f32[128,128]{1,0:T(8,128)S(1)} custom-call(f32[128,128]{1,0:T(8,128)S(1)} %convolution_subtract_fusion.2), custom_call_target="Cholesky" | custom-call | tf_op jit(solution)/shard_map/jit(cholesky)/cholesky | solution.py:47
  527.5 0.7 compare_reduce_fusion.2
  528.2 0.6 compare_reduce_fusion.3
  528.9 0.6 compare_reduce_fusion.1
  529.5 0.7 compare_reduce_fusion
  532.8 11.3 %while.1 = (s32[]{:T(128)}, f32[512,512]{0,1:T(8,128)S(1)}, s32[4,2]{0,1:T(2,128)S(1)}, f32[4,128,128]{2,1,0:T(8,128)}, s32[]{:T(128)}) while((s32[]{:T(128)}, f32[512,512]{0,1:T(8,128)S(1)}, s32[4,2]{0,1:T(2,128)S(1)}, f32[4,128,128]{2,1,0:T(8,128)}, s32[]{:T(128)}) %tuple.39), condition=%wide.while_cond, body=%wide.while_body.sunk | while | flops 2 | bytes 393829 | solution.py:49
  532.9 0.6 fusion.100
  533.5 1.4 dynamic-slice.9
  535.0 0.6 bitcast_dynamic-update-slice_fusion.4
  535.7 0.6 fusion.100
  536.3 1.4 dynamic-slice.9
  537.9 0.6 bitcast_dynamic-update-slice_fusion.4
  539.2 1.4 dynamic-slice.9
  540.7 0.6 bitcast_dynamic-update-slice_fusion.4
  541.4 0.6 fusion.100
  542.0 1.4 dynamic-slice.9
  543.5 0.6 bitcast_dynamic-update-slice_fusion.4
  544.1 40.1 %custom-call.35 = f32[4,128,128]{1,2,0:T(8,128)S(1)} custom-call(f32[4,128,128]{2,1,0:T(8,128)} %get-tuple-element.9), custom_call_target="InvertDiagBlocksLowerTriangular" | custom-call | tf_op jit(solution)/shard_map/triangular_solve | solution.py:49
  587.6 128.5 %psum.31 = f32[4608]{0:T(1024)S(1)} all-reduce(f32[4608]{0:T(1024)S(1)} %convolution_reduce_fusion), channel_id=1, replica_groups=mesh['samp'=32,'par'=16] {'samp'}, use_global_device_ids=true, to_apply=%region_13.14 | all-reduce | flops 4608 | bytes 36864 | tf_op jit(solution)/shard_map/psum | solution.py:77
  716.0 0.6 reshape.150
  (89 shorter events, 10.4 us)
Async XLA Ops:
  7.2 24.9 %copy-start = (bf16[16,2,64,256]{3,2,1,0:T(8,128)(2,1)S(1)}, bf16[16,2,64,256]{3,2,1,0:T(8,128)(2,1)}, u32[]{:S(2)}) copy-start(bf16[16,2,64,256]{3,2,1,0:T(8,128)(2,1)} %param.3) | copy-start | bytes 3145732
  7.2 329.1 %all-gather.3.cloned.1.call-start = ((), (), s32[]{:S(2)}) async-start(), calls=%async_computation.1 | async-start | bytes 4866048 | tf_op jit(solution)/shard_map/all_gather | solution.py:65
  9.5 4.6 copy-start.7
  14.5 4.0 copy-start.2
  14.5 5.1 copy-start.3
  14.5 5.1 copy-start.4
  14.5 5.1 copy-start.5
  14.5 5.1 copy-start.6
  32.0 3.7 copy-start.9
  404.7 33.8 %all-to-all-start = ((f32[32,16,512]{2,1,0:T(8,128)}), f32[32,16,512]{2,1,0:T(8,128)}, u32[]{:S(2)}, u32[]{:S(2)}) async-start(f32[32,16,512]{2,1,0:T(8,128)} %stack.32), calls=%async_computation | async-start | bytes 2097152 | tf_op jit(solution)/shard_map/all_to_all | solution.py:16
  442.9 1.0 copy-start.1
  587.3 129.4 %copy-start.8 = (f32[16,1]{0,1:T(1,128)}, f32[16,1]{0,1:T(1,128)S(1)}, u32[]{:S(2)}) copy-start(f32[16,1]{0,1:T(1,128)S(1)} %fusion.59) | copy-start | bytes 196
Sparse Core Ops, SparseCore 0:
  247.6 88.6 all-gather.2
